TPU v7x, 32 devices: a whole 2x2x4 slice. The times are simulated.
32 devices in a mesh: row: 4 (over y, x), blk: 8 (over z, core).
Axes of the slice: x: 2, y: 2, z: 4, core: 2. Of those that a mesh axis runs over, the one named last changes fastest.
Arguments:
- features: bfloat16 [8192, 512], P(('row', 'blk')), may hold values from -6 to 6
- edge_tiles: bfloat16 [4, 8, 48, 128, 128], P('row', 'blk'), may hold values from 0 to 1
- tile_src: int32 [4, 8, 48], P('row', 'blk'), may hold values from 0 to 15, as said below
- tile_dst: int32 [4, 8, 48], P('row', 'blk'), may hold values from 0 to 7
- tile_count: int32 [4, 8], P('row', 'blk'), may hold values from 9 to 48, as said below
- weight: bfloat16 [1024, 512], replicated, may hold values from -0.25 to 0.25
- out_bias: float32 [512], replicated, may hold values from -3 to 3
Outputs:
- exposure: bfloat16 [8192, 512], P(('row', 'blk'))
Inputs may be any that keep to these rules, and one draw needn't show every extreme that they name: `tile_count`: live slots of a device; the busiest device has all 48. `tile_src`: the live entries of each device ascend; source block s lies at loop position s // 2, which may be any position of the closed loop of 8 positions.
All inputs are finite; a program needn't handle non-finite values.
Results may differ from a plain program's by a relative error of at most 0.006.
Values may be sent and summed in bfloat16 or wider, within the bound.
A program may use at most 128 MiB of HBM per device.

v0:
```python
import jax
import jax.numpy as jnp
from jax import lax
from jax.sharding import PartitionSpec as P


def accumulate(table, block_of, tiles_here, target_ids, live_slot, dest_blocks):
    slot_total = tiles_here.shape[0]
    tile_width = tiles_here.shape[-1]
    feat_width = table.shape[1]
    table_blocks = table.reshape(-1, tile_width, feat_width)
    source_total = table_blocks.shape[0]
    step_size = 16
    rounds = slot_total // step_size
    source_ids = jnp.arange(source_total, dtype=jnp.int32)
    dest_ids = jnp.arange(dest_blocks, dtype=jnp.int32)

    def one_round(index, totals):
        first = index * step_size
        tiles = lax.dynamic_slice_in_dim(tiles_here, first, step_size, 0)
        blocks = lax.dynamic_slice_in_dim(block_of, first, step_size, 0)
        targets = lax.dynamic_slice_in_dim(target_ids, first, step_size, 0)
        live = lax.dynamic_slice_in_dim(live_slot, first, step_size, 0)
        one_hot = (blocks[:, None] == source_ids[None, :]).astype(jnp.bfloat16)
        picked = jnp.einsum(
            "tk,kif->tif", one_hot, table_blocks, preferred_element_type=jnp.float32
        ).astype(jnp.bfloat16)
        products = jnp.einsum("tij,tjf->tif", tiles, picked, preferred_element_type=jnp.float32)
        selector = ((targets[None, :] == dest_ids[:, None]) & live[None, :]).astype(jnp.float32)
        return totals + jnp.einsum(
            "qt,tif->qif", selector, products, precision=lax.Precision.HIGHEST
        )

    empty = jnp.zeros((dest_blocks, tile_width, feat_width), jnp.float32)
    return lax.fori_loop(0, rounds, one_round, empty)


def per_device(features, edge_tiles, tile_src, tile_dst, tile_count, weight, out_bias):
    tiles_here = edge_tiles[0, 0]
    source_ids = tile_src[0, 0]
    target_ids = tile_dst[0, 0]
    live_count = tile_count[0, 0]
    slot_total = tiles_here.shape[0]
    tile_width = tiles_here.shape[-1]
    node_rows = features.shape[0]
    feat_width = features.shape[1]
    group_count = lax.axis_size("row")
    dest_blocks = group_count * node_rows // tile_width
    slot_ids = jnp.arange(slot_total, dtype=jnp.int32)
    live_slot = slot_ids < live_count
    table = lax.all_gather(features, "blk", axis=0, tiled=True)
    totals = accumulate(table, source_ids, tiles_here, target_ids, live_slot, dest_blocks).reshape(
        -1, feat_width
    )
    row_sums = jnp.sum(tiles_here, axis=2, dtype=jnp.float32)
    block_ids = jnp.arange(dest_blocks, dtype=jnp.int32)
    selector = ((target_ids[None, :] == block_ids[:, None]) & live_slot[None, :]).astype(
        jnp.float32
    )
    degree_part = jnp.dot(selector, row_sums, precision=lax.Precision.HIGHEST).reshape(-1)
    aggregate, degree = (
        lax.psum_scatter(
            totals.astype(jnp.bfloat16), "row", scatter_dimension=0, tiled=True
        ).astype(jnp.float32),
        lax.psum_scatter(
            degree_part.astype(jnp.bfloat16), "row", scatter_dimension=0, tiled=True
        ).astype(jnp.float32),
    )
    neighbor_mean = (aggregate / jnp.maximum(degree, 1.0)[:, None]).astype(jnp.bfloat16)
    joined = jnp.concatenate([features, neighbor_mean], axis=1)
    mixed = jnp.dot(joined, weight, preferred_element_type=jnp.float32) + out_bias
    return jax.nn.relu(mixed).astype(jnp.bfloat16)


def solution(mesh):
    in_specs = (
        P(("row", "blk"), None),
        P("row", "blk", None, None, None),
        P("row", "blk", None),
        P("row", "blk", None),
        P("row", "blk"),
        P(),
        P(),
    )
    out_specs = P(("row", "blk"), None)
    return jax.shard_map(
        per_device, mesh=mesh, in_specs=in_specs, out_specs=out_specs, check_vma=False
    )
```

profile of v0, /device:TPU:0, one launch (start us, length us, event | category | flops | bytes accessed | tf_op | source)
XLA Modules:
  0.0 129.2 jit_solution(11049505281381869969)
XLA Ops:
  6.5 0.7 all-gather.2.cloned.1.call-update
  7.3 0.0 reduce-scatter.2.cloned.1.call-start
  8.0 32.8 %all-gather.2.cloned.1.call-done = bf16[2048,512]{1,0:T(8,128)(2,1)} async-done(((bf16[256,512]{1,0:T(8,128)(2,1)}), bf16[2048,512]{1,0:T(8,128)(2,1)}) %all-gather.2.cloned.1.call-update) | async-done | bytes 2097168 | tf_op jit(solution)/shard_map/all_gather | solution.py:51
  40.8 4.1 %copy.14 = bf16[16,128,512]{2,0,1:T(8,128)(2,1)} copy(bf16[16,128,512]{2,1,0:T(8,128)(2,1)} %bitcast.29) | data formatting | bytes 4194304
  44.9 45.7 %while.14 = (s32[]{:T(128)}, f32[8,128,512]{2,0,1:T(8,128)S(1)}, s32[48]{0:T(128)S(1)}, pred[48]{0:T(512)(128)(4,1)S(1)}, bf16[48,128,128]{2,1,0:T(8,128)(2,1)},...) while((s32[]{:T(128)}, f32[8,128,512]{2,0,1:T(8,128)S(1)}, ...), condition=%wide.region_1.0_spmd.clone, body=%wide.region_0.0_spmd.clone.sunk | while | flops 404750848 | bytes 19399268 | solution.py:35
  44.9 0.1 dynamic_slice.39
  45.0 2.3 %convolution_convert_fusion.3 = bf16[16,128,512]{2,0,1:T(8,128)(2,1)S(1)} fusion(bf16[16,128,512]{2,0,1:T(8,128)(2,1)} %get-tuple-element.280, s32[16]{0:T(128)S(1)} %dynamic_slice.39), kind=kOutput, calls=%fused_computation.7.clone.1 | convolution fusion | flops 34603264 | bytes 4194368 | tf_op jit(solution)/shard_map/while/body/eval_jaxpr/tk,kif->tif/dot_general | solution.py:25
  47.3 5.6 %fusion.47 = f32[16,128,512]{2,1,0:T(8,128)} fusion(bf16[16,128,512]{2,0,1:T(8,128)(2,1)S(1)} %convolution_convert_fusion.3, bf16[48,128,128]{2,1,0:T(8,128)(2,1)} %get-tuple-element.278, s32[]{:T(128)S(6)} %select_n.12), kind=kOutput, calls=%fused_computation.4.clone.1 | convolution fusion | flops 268435456 | bytes 6815748 | tf_op jit(solution)/shard_map/while/body/eval_jaxpr/tij,tjf->tif/dot_general | solution.py:28
  52.9 0.1 dynamic_slice.40
  53.0 0.1 dynamic_slice.41
  53.1 7.0 %select_add_fusion.2 = f32[8,128,512]{2,0,1:T(8,128)S(1)} fusion(f32[8,128,512]{2,0,1:T(8,128)S(1)} %get-tuple-element.264, f32[16,128,512]{2,1,0:T(8,128)} %fusion.47, pred[]{:T(512)S(6)} %compare.3, s32[16]{0:T(128)S(1)} %dynamic_slice.40, pred[16]{0:T(512)(128)(4,1)S(1)} %dynamic_slice.41), kind=kOutput, calls=%fused_computation.6.clone.1 | convolution fusion | flops 101712128 | bytes 8388689 | tf_op jit(solution)/shard_map/while/body/eval_jaxpr/qt,tif->qif/dot_general | solution.py:30
  60.1 0.1 dynamic_slice.39
  60.2 2.3 %convolution_convert_fusion.3 = bf16[16,128,512]{2,0,1:T(8,128)(2,1)S(1)} fusion(bf16[16,128,512]{2,0,1:T(8,128)(2,1)} %get-tuple-element.280, s32[16]{0:T(128)S(1)} %dynamic_slice.39), kind=kOutput, calls=%fused_computation.7.clone.1 | convolution fusion | flops 34603264 | bytes 4194368 | tf_op jit(solution)/shard_map/while/body/eval_jaxpr/tk,kif->tif/dot_general | solution.py:25
  62.6 5.6 %fusion.47 = f32[16,128,512]{2,1,0:T(8,128)} fusion(bf16[16,128,512]{2,0,1:T(8,128)(2,1)S(1)} %convolution_convert_fusion.3, bf16[48,128,128]{2,1,0:T(8,128)(2,1)} %get-tuple-element.278, s32[]{:T(128)S(6)} %select_n.12), kind=kOutput, calls=%fused_computation.4.clone.1 | convolution fusion | flops 268435456 | bytes 6815748 | tf_op jit(solution)/shard_map/while/body/eval_jaxpr/tij,tjf->tif/dot_general | solution.py:28
  68.2 0.1 dynamic_slice.40
  68.2 0.1 dynamic_slice.41
  68.3 7.0 %select_add_fusion.2 = f32[8,128,512]{2,0,1:T(8,128)S(1)} fusion(f32[8,128,512]{2,0,1:T(8,128)S(1)} %get-tuple-element.264, f32[16,128,512]{2,1,0:T(8,128)} %fusion.47, pred[]{:T(512)S(6)} %compare.3, s32[16]{0:T(128)S(1)} %dynamic_slice.40, pred[16]{0:T(512)(128)(4,1)S(1)} %dynamic_slice.41), kind=kOutput, calls=%fused_computation.6.clone.1 | convolution fusion | flops 101712128 | bytes 8388689 | tf_op jit(solution)/shard_map/while/body/eval_jaxpr/qt,tif->qif/dot_general | solution.py:30
  75.4 0.1 dynamic_slice.39
  75.4 2.3 %convolution_convert_fusion.3 = bf16[16,128,512]{2,0,1:T(8,128)(2,1)S(1)} fusion(bf16[16,128,512]{2,0,1:T(8,128)(2,1)} %get-tuple-element.280, s32[16]{0:T(128)S(1)} %dynamic_slice.39), kind=kOutput, calls=%fused_computation.7.clone.1 | convolution fusion | flops 34603264 | bytes 4194368 | tf_op jit(solution)/shard_map/while/body/eval_jaxpr/tk,kif->tif/dot_general | solution.py:25
  77.8 5.6 %fusion.47 = f32[16,128,512]{2,1,0:T(8,128)} fusion(bf16[16,128,512]{2,0,1:T(8,128)(2,1)S(1)} %convolution_convert_fusion.3, bf16[48,128,128]{2,1,0:T(8,128)(2,1)} %get-tuple-element.278, s32[]{:T(128)S(6)} %select_n.12), kind=kOutput, calls=%fused_computation.4.clone.1 | convolution fusion | flops 268435456 | bytes 6815748 | tf_op jit(solution)/shard_map/while/body/eval_jaxpr/tij,tjf->tif/dot_general | solution.py:28
  83.4 0.1 dynamic_slice.40
  83.5 0.1 dynamic_slice.41
  83.5 7.0 %select_add_fusion.2 = f32[8,128,512]{2,0,1:T(8,128)S(1)} fusion(f32[8,128,512]{2,0,1:T(8,128)S(1)} %get-tuple-element.264, f32[16,128,512]{2,1,0:T(8,128)} %fusion.47, pred[]{:T(512)S(6)} %compare.3, s32[16]{0:T(128)S(1)} %dynamic_slice.40, pred[16]{0:T(512)(128)(4,1)S(1)} %dynamic_slice.41), kind=kOutput, calls=%fused_computation.6.clone.1 | convolution fusion | flops 101712128 | bytes 8388689 | tf_op jit(solution)/shard_map/while/body/eval_jaxpr/qt,tif->qif/dot_general | solution.py:30
  90.6 2.1 %copy.23 = bf16[8,128,512]{2,1,0:T(8,128)(2,1)} copy(f32[8,128,512]{2,0,1:T(8,128)S(1)} %get-tuple-element.159) | data formatting | bytes 3145728 | tf_op jit(solution)/shard_map/while | solution.py:35
  92.7 0.6 dynamic-slice
  94.0 1.9 %convert_reduce_fusion = f32[48,128]{1,0:T(8,128)S(1)} fusion(bf16[1,1,48,128,128]{4,3,2,1,0:T(8,128)(2,1)} %bitcast.27), kind=kLoop, calls=%fused_computation.18 | loop fusion | flops 1566720 | bytes 1597440 | tf_op jit(solution)/shard_map/reduce_sum | solution.py:55
  95.8 0.1 fusion.22
  96.0 10.1 %all-reduce = bf16[1024]{0:T(1024)(128)(2,1)S(1)} all-reduce(bf16[1024]{0:T(1024)(128)(2,1)S(1)} %fusion.22), channel_id=3, replica_groups=mesh['row'=4,'blk'=8] {'row'}, use_global_device_ids=true, to_apply=%region_4.0.clone | all-reduce | flops 1024 | bytes 4096
  106.1 0.1 convert_maximum_fusion
  106.1 14.0 %reduce-scatter.2.cloned.1.call-done = bf16[256,512]{1,0:T(8,128)(2,1)} async-done(((bf16[1024,512]{1,0:T(8,128)(2,1)}), bf16[256,512]{1,0:T(8,128)(2,1)}) %reduce-scatter.2.cloned.1.call-update) | async-done | bytes 262160 | tf_op jit(solution)/shard_map/reduce_scatter | solution.py:62
  120.1 1.1 divide_convert_fusion
  121.2 1.1 fusion.21
  (16 shorter events, 0.1 us)
Async XLA Ops:
  6.5 114.6 %copy-start = (bf16[1024,512]{1,0:T(8,128)(2,1)S(1)}, bf16[1024,512]{1,0:T(8,128)(2,1)}, u32[]{:S(2)}) copy-start(bf16[1024,512]{1,0:T(8,128)(2,1)} %param.14) | copy-start | bytes 3145732
  6.5 34.3 %all-gather.2.cloned.1.call-start = ((), (), s32[]{:S(2)}) async-start(), calls=%async_computation.1 | async-start | bytes 2359296 | tf_op jit(solution)/shard_map/all_gather | solution.py:51
  7.3 112.8 %reduce-scatter.2.cloned.1.call-start = ((), (), s32[]{:S(2)}) async-start(), calls=%async_computation.2 | async-start | bytes 1310720 | tf_op jit(solution)/shard_map/reduce_scatter | solution.py:62
  40.8 4.1 %copy-start.2 = (s32[1,1,48]{2,1,0:T(1,128)S(1)}, s32[1,1,48]{2,1,0:T(1,128)}, u32[]{:S(2)}) copy-start(s32[1,1,48]{2,1,0:T(1,128)} %param.12) | copy-start | bytes 580
  40.8 4.1 %copy-start.4 = (s32[1,1,48]{2,1,0:T(1,128)S(1)}, s32[1,1,48]{2,1,0:T(1,128)}, u32[]{:S(2)}) copy-start(s32[1,1,48]{2,1,0:T(1,128)} %param.11) | copy-start | bytes 580
  90.6 2.1 %copy-start.5 = (u32[32]{0:T(128)S(1)}, u32[32]{0:T(128)}, u32[]{:S(2)}) copy-start(u32[32]{0:T(128)} %constant.43) | copy-start | bytes 388
  92.7 28.5 %copy-start.1 = (bf16[256,512]{1,0:T(8,128)(2,1)S(1)}, bf16[256,512]{1,0:T(8,128)(2,1)}, u32[]{:S(2)}) copy-start(bf16[256,512]{1,0:T(8,128)(2,1)} %param.9) | copy-start | bytes 786436
  92.7 28.5 %copy-start.3 = (f32[512]{0:T(512)S(1)}, f32[512]{0:T(512)}, u32[]{:S(2)}) copy-start(f32[512]{0:T(512)} %param.15) | copy-start | bytes 6148
Sparse Core Ops, SparseCore 0:
  9.0 31.7 all-gather.1
  92.8 27.2 reduce-scatter.1
where the time goes:
time: 130 us; the launch traced here: 129 us
  waiting for transfers between devices  47.5 us (37%)
  matrix products  46.2 us (36%)
  between operations  14.8 us (11%)
  blocking collectives  10.1 us (8%)
  local copies, waits for them, and re-layouts  7.47 us (6%)
  other arithmetic  3.04 us (2%)
    all_gather x1, waiting for transfers between devices, per_device(): table = lax.all_gather(features, 'blk', axis=0, tiled=True)  32.8 us
    dot_general x3, matrix products, one_round(): jnp.einsum('qt,tif->qif', selector, products, precision=lax.Precision.HIG...  21.1 us
    dot_general x3, matrix products, one_round(): jnp.einsum('tij,tjf->tif', tiles, picked, preferred_element_type=jnp.floa...  16.8 us
    reduce_scatter x1, waiting for transfers between devices, per_device(): lax.psum_scatter(totals.astype(jnp.bfloat16), 'row', scatter_dimension=0,...  14 us
    unnamed x1, blocking collectives  10.1 us
    dot_general x3, matrix products, one_round(): jnp.einsum('tk,kif->tif', one_hot, table_blocks, preferred_element_type=j...  7.02 us
    unnamed x14, local copies, waits for them, and re-layouts  4.71 us
  transfers between devices with their start and end apart: 2, of which 2 were waited for; matrix products, arithmetic and copies ran while one was open for 2% of the time, Pallas kernels for 0%

commit v1 on v0

--- a/solution.py
+++ b/solution.py
@@ -1,7 +1,386 @@
+import functools
+
 import jax
 import jax.numpy as jnp
 from jax import lax
+from jax.experimental import pallas as pl
+from jax.experimental.pallas import tpu as pltpu
 from jax.sharding import PartitionSpec as P
+
+MESH = pl.DeviceIdType.MESH
+CHUNK = 128
+AHEAD = 3
+DENSE_LIMIT = 12 * 2**20
+
+
+def fused(
+    rows_n, spots, live_ref, src_ref, dst_ref, feat_hbm, tiles_hbm, weight_hbm, bias_ref, out_ref,
+    tab, tiles, chain, dense, weight, mine, acc, mixed, send_buf, recv_buf, lists, list_smem,
+    in_sem, own_sem, left_sem, right_sem, side_sem, line_recv, side_recv, row_send, row_recv,
+):
+    slots = tiles.shape[0]
+    width = tiles.shape[-1]
+    chunks = tab.shape[0]
+    node_rows = mine.shape[0]
+    feat = mine.shape[1]
+    per_node = node_rows // width
+    sources = spots * 2 * per_node
+    dests = rows_n * per_node
+    wide = 2 * per_node
+    row = lax.axis_index("row")
+    blk = lax.axis_index("blk")
+    z = blk // 2
+    c = blk % 2
+    side = z * 2 + (1 - c)
+
+    loads = [
+        pltpu.make_async_copy(tiles_hbm, tiles, in_sem.at[0]),
+        pltpu.make_async_copy(feat_hbm, mine, in_sem.at[1]),
+        pltpu.make_async_copy(weight_hbm, weight, in_sem.at[2]),
+    ]
+    for load in loads:
+        load.start()
+
+    barrier = pltpu.get_barrier_semaphore()
+
+    def greet(r, b):
+        pl.semaphore_signal(barrier, inc=1, device_id=(r, b), device_id_type=MESH)
+
+    @pl.when(z > 0)
+    def _():
+        greet(row, blk - 2)
+
+    @pl.when(z < spots - 1)
+    def _():
+        greet(row, blk + 2)
+
+    greet(row, side)
+    for step in range(1, rows_n):
+        greet((row + step) % rows_n, blk)
+
+    def own_local(k):
+        return pltpu.make_async_copy(
+            feat_hbm.at[:, pl.ds(pl.multiple_of(k * CHUNK, CHUNK), CHUNK)], tab.at[k, z, c], own_sem.at[k]
+        )
+
+    def line_copy(k, p, step, sems, own):
+        slot = tab.at[k, p, c]
+        source = feat_hbm.at[:, pl.ds(pl.multiple_of(k * CHUNK, CHUNK), CHUNK)] if own else slot
+        return pltpu.make_async_remote_copy(
+            src_ref=source, dst_ref=slot, send_sem=sems.at[k, p], recv_sem=line_recv.at[k, p],
+            device_id=(row, blk + 2 * step), device_id_type=MESH,
+        )
+
+    def side_copy(k, p, own):
+        slot = tab.at[k, p, c]
+        source = feat_hbm.at[:, pl.ds(pl.multiple_of(k * CHUNK, CHUNK), CHUNK)] if own else slot
+        return pltpu.make_async_remote_copy(
+            src_ref=source, dst_ref=slot, send_sem=side_sem.at[k, p], recv_sem=side_recv.at[k, p],
+            device_id=(row, side), device_id_type=MESH,
+        )
+
+    def side_arrival(k, p):
+        slot = tab.at[k, p, 1 - c]
+        return pltpu.make_async_remote_copy(
+            src_ref=slot, dst_ref=slot, send_sem=side_sem.at[k, p], recv_sem=side_recv.at[k, p],
+            device_id=(row, side), device_id_type=MESH,
+        )
+
+    def row_copy(k, step):
+        peer = (row + step) % rows_n
+        return pltpu.make_async_remote_copy(
+            src_ref=send_buf.at[k, peer], dst_ref=recv_buf.at[k, row],
+            send_sem=row_send.at[k, peer], recv_sem=row_recv.at[k, row],
+            device_id=(peer, blk), device_id_type=MESH,
+        )
+
+    def row_arrival(k, step):
+        peer = (row + step) % rows_n
+        return pltpu.make_async_remote_copy(
+            src_ref=send_buf.at[k, peer], dst_ref=recv_buf.at[k, peer],
+            send_sem=row_send.at[k, peer], recv_sem=row_recv.at[k, peer],
+            device_id=(peer, blk), device_id_type=MESH,
+        )
+
+    def send_own(k):
+        @pl.when(z > 0)
+        def _():
+            line_copy(k, z, -1, left_sem, True).start()
+
+        @pl.when(z < spots - 1)
+        def _():
+            line_copy(k, z, 1, right_sem, True).start()
+
+        side_copy(k, z, True).start()
+
+    greeted = (
+        jnp.where(z > 0, 1, 0) + jnp.where(z < spots - 1, 1, 0) + rows_n
+    )
+    pl.semaphore_wait(barrier, greeted)
+
+    def first_sends(k, carry):
+        send_own(k)
+        own_local(k).start()
+        return carry
+
+    lax.fori_loop(0, min(AHEAD, chunks), first_sends, 0)
+
+    list_rows = lists.shape[0] - 1
+    lane = lax.broadcasted_iota(jnp.int32, (1, 128), 1)
+    place = lax.broadcasted_iota(jnp.int32, (list_rows, 128), 0) * 128 + lax.broadcasted_iota(
+        jnp.int32, (list_rows, 128), 1
+    )
+    live = live_ref[0, 0]
+
+    def one_key(t, carry):
+        keys, last = carry
+        key = dst_ref[0, t] * sources + src_ref[0, t]
+        key = jnp.where(t < live, key, -1)
+        return jnp.where(lane == t, key, keys), jnp.where(place == key, t, last)
+
+    keys, last = lax.fori_loop(
+        0, slots, one_key,
+        (jnp.full((1, 128), -1, jnp.int32), jnp.full((list_rows, 128), slots, jnp.int32)), unroll=8,
+    )
+
+    def one_before(u, before):
+        key = dst_ref[0, u] * sources + src_ref[0, u]
+        key = jnp.where(u < live, key, -2)
+        return jnp.where((keys == key) & (lane > u), u, before)
+
+    before = lax.fori_loop(0, slots, one_before, jnp.full((1, 128), slots, jnp.int32), unroll=8)
+    lists[pl.ds(0, list_rows), :] = last
+    lists[pl.ds(list_rows, 1), :] = before
+    to_smem = pltpu.make_async_copy(lists, list_smem, in_sem.at[3])
+    to_smem.start()
+    chain[slots] = jnp.zeros((width, width), jnp.float32)
+    loads[0].wait()
+    to_smem.wait()
+
+    def one_link(t, carry):
+        chain[t] = tiles[t].astype(jnp.float32) + chain[list_smem[list_rows, t]]
+        return carry
+
+    lax.fori_loop(0, slots, one_link, 0, unroll=4)
+
+    def one_dest(q, carry):
+        for s in range(sources):
+            at = q * sources + s
+            block = chain[list_smem[at // 128, at % 128]]
+            dense[s // wide, pl.ds(pl.multiple_of(q * width, width), width), pl.ds(s % wide * width, width)] = (
+                block.astype(jnp.bfloat16)
+            )
+        return carry
+
+    lax.fori_loop(0, dests, one_dest, 0)
+
+    def consume(k, p, first):
+        block = tab[k, p].reshape(wide * width, CHUNK)
+        product = jnp.dot(dense[p], block, preferred_element_type=jnp.float32)
+        if first:
+            acc[k] = product
+        else:
+            acc[k] += product
+
+    def send_rows(k, values):
+        send_buf[k] = values.astype(jnp.bfloat16).reshape(rows_n, node_rows, CHUNK)
+        for step in range(1, rows_n):
+            row_copy(k, step).start()
+
+    def gather_rows(k):
+        total = send_buf[k, row].astype(jnp.float32)
+        for step in range(1, rows_n):
+            row_arrival(k, step).wait_recv()
+            total += recv_buf[k, (row + step) % rows_n].astype(jnp.float32)
+        return total
+
+    def step_body(s, carry):
+        @pl.when(s + AHEAD < chunks)
+        def _():
+            send_own(s + AHEAD)
+            own_local(s + AHEAD).start()
+
+        for h in range(1, spots):
+            k = s - (h - 1)
+            inside = (k >= 0) & (k < chunks)
+
+            @pl.when(inside & (z + h < spots))
+            def _():
+                line_copy(k, z + h, -1, left_sem, False).wait_recv()
+
+                @pl.when(z > 0)
+                def _():
+                    line_copy(k, z + h, -1, left_sem, False).start()
+
+                side_copy(k, z + h, False).start()
+
+            @pl.when(inside & (z - h >= 0))
+            def _():
+                line_copy(k, z - h, 1, right_sem, False).wait_recv()
+
+                @pl.when(z < spots - 1)
+                def _():
+                    line_copy(k, z - h, 1, right_sem, False).start()
+
+                side_copy(k, z - h, False).start()
+
+        @pl.when(s == 0)
+        def _():
+            ones = jnp.ones((wide * width, CHUNK), jnp.bfloat16)
+            total = jnp.dot(dense[0], ones, preferred_element_type=jnp.float32)
+            for p in range(1, spots):
+                total += jnp.dot(dense[p], ones, preferred_element_type=jnp.float32)
+            send_rows(chunks, total)
+
+        @pl.when(s == 1)
+        def _():
+            loads[1].wait()
+            loads[2].wait()
+            mixed[...] = (
+                jnp.dot(mine[...], weight[pl.ds(0, feat), :], preferred_element_type=jnp.float32) + bias_ref[...]
+            )
+
+        for h in range(spots):
+            k = s - h
+            inside = (k >= 0) & (k < chunks)
+            if h == 0:
+
+                @pl.when(inside)
+                def _():
+                    own_local(k).wait()
+                    side_arrival(k, z).wait_recv()
+                    consume(k, z, True)
+
+            else:
+
+                @pl.when(inside & (z + h < spots))
+                def _():
+                    side_arrival(k, z + h).wait_recv()
+                    consume(k, z + h, False)
+
+                @pl.when(inside & (z - h >= 0))
+                def _():
+                    side_arrival(k, z - h).wait_recv()
+                    consume(k, z - h, False)
+
+        ready = s - (spots - 1)
+
+        @pl.when((ready >= 0) & (ready < chunks))
+        def _():
+            send_rows(ready, acc[ready])
+
+        arrived = s - spots
+
+        @pl.when(arrived == 0)
+        def _():
+            acc[0, pl.ds(0, node_rows), :] = jnp.maximum(gather_rows(chunks), 1.0)
+
+        @pl.when(arrived >= 0)
+        def _():
+            mean = (gather_rows(arrived) / acc[0, pl.ds(0, node_rows), :]).astype(jnp.bfloat16)
+            part = weight[pl.ds(pl.multiple_of(feat + arrived * CHUNK, CHUNK), CHUNK), :]
+            mixed[...] += jnp.dot(mean, part, preferred_element_type=jnp.float32)
+
+        return carry
+
+    lax.fori_loop(0, chunks + spots, step_body, 0)
+    out_ref[...] = jnp.maximum(mixed[...], 0.0).astype(jnp.bfloat16)
+
+    def finish(k, carry):
+        side_copy(k, z, True).wait_send()
+
+        @pl.when(z > 0)
+        def _():
+            line_copy(k, z, -1, left_sem, True).wait_send()
+
+        @pl.when(z < spots - 1)
+        def _():
+            line_copy(k, z, 1, right_sem, True).wait_send()
+
+        for h in range(1, spots):
+
+            @pl.when(z + h < spots)
+            def _():
+                side_copy(k, z + h, False).wait_send()
+
+                @pl.when(z > 0)
+                def _():
+                    line_copy(k, z + h, -1, left_sem, False).wait_send()
+
+            @pl.when(z - h >= 0)
+            def _():
+                side_copy(k, z - h, False).wait_send()
+
+                @pl.when(z < spots - 1)
+                def _():
+                    line_copy(k, z - h, 1, right_sem, False).wait_send()
+
+        return carry
+
+    lax.fori_loop(0, chunks, finish, 0)
+
+    def finish_rows(k, carry):
+        for step in range(1, rows_n):
+            row_copy(k, step).wait_send()
+        return carry
+
+    lax.fori_loop(0, chunks + 1, finish_rows, 0)
+
+
+def per_device_fused(features, edge_tiles, tile_src, tile_dst, tile_count, weight, out_bias):
+    rows_n = lax.axis_size("row")
+    spots = lax.axis_size("blk") // 2
+    slots, width = edge_tiles.shape[2], edge_tiles.shape[-1]
+    node_rows, feat = features.shape
+    chunks = feat // CHUNK
+    per_node = node_rows // width
+    dests, sources = rows_n * per_node, spots * 2 * per_node
+    list_rows = -(-dests * sources // 128)
+    dest_rows = rows_n * node_rows
+    hbm = pl.BlockSpec(memory_space=pl.ANY)
+    smem = pl.BlockSpec(memory_space=pltpu.SMEM)
+    vmem = pl.BlockSpec(memory_space=pltpu.VMEM)
+    dma = pltpu.SemaphoreType.DMA
+    return pl.pallas_call(
+        functools.partial(fused, rows_n, spots),
+        out_shape=jax.ShapeDtypeStruct((node_rows, feat), jnp.bfloat16),
+        in_specs=[smem, smem, smem, hbm, hbm, hbm, vmem],
+        out_specs=vmem,
+        scratch_shapes=[
+            pltpu.VMEM((chunks, spots, 2, node_rows, CHUNK), jnp.bfloat16),
+            pltpu.VMEM((slots, width, width), jnp.bfloat16),
+            pltpu.VMEM((slots + 1, width, width), jnp.float32),
+            pltpu.VMEM((spots, dest_rows, 2 * node_rows), jnp.bfloat16),
+            pltpu.VMEM(weight.shape, jnp.bfloat16),
+            pltpu.VMEM((node_rows, feat), jnp.bfloat16),
+            pltpu.VMEM((chunks, dest_rows, CHUNK), jnp.float32),
+            pltpu.VMEM((node_rows, feat), jnp.float32),
+            pltpu.VMEM((chunks + 1, rows_n, node_rows, CHUNK), jnp.bfloat16),
+            pltpu.VMEM((chunks + 1, rows_n, node_rows, CHUNK), jnp.bfloat16),
+            pltpu.VMEM((list_rows + 1, 128), jnp.int32),
+            pltpu.SMEM((list_rows + 1, 128), jnp.int32),
+            dma((4,)),
+            dma((chunks,)),
+            dma((chunks, spots)),
+            dma((chunks, spots)),
+            dma((chunks, spots)),
+            dma((chunks, spots)),
+            dma((chunks, spots)),
+            dma((chunks + 1, rows_n)),
+            dma((chunks + 1, rows_n)),
+        ],
+        compiler_params=pltpu.CompilerParams(
+            collective_id=0, has_side_effects=True, vmem_limit_bytes=48 * 2**20
+        ),
+    )(
+        tile_count,
+        tile_src.reshape(1, slots),
+        tile_dst.reshape(1, slots),
+        features,
+        edge_tiles.reshape(slots, width, width),
+        weight,
+        out_bias.reshape(1, feat),
+    )
 
 
 def accumulate(table, block_of, tiles_here, target_ids, live_slot, dest_blocks):
@@ -83,6 +462,12 @@
         P(),
     )
     out_specs = P(("row", "blk"), None)
+
+    def body(features, edge_tiles, *rest):
+        dense = 2 * lax.axis_size("row") * lax.axis_size("blk") * features.shape[0] ** 2
+        run = per_device_fused if dense <= DENSE_LIMIT else per_device
+        return run(features, edge_tiles, *rest)
+
     return jax.shard_map(
-        per_device, mesh=mesh, in_specs=in_specs, out_specs=out_specs, check_vma=False
-    )
+        body, mesh=mesh, in_specs=in_specs, out_specs=out_specs, check_vma=False
+    )

time: 130 us -> 46.6 us (0.36)
  waiting for transfers between devices: 47.5 us -> 0 us
  matrix products: 46.2 us -> 0 us
  Pallas kernels: 0 us -> 39.4 us
  between operations: 14.8 us -> 0.67 us
  blocking collectives: 10.1 us -> 0 us
  other arithmetic: 3.04 us -> 0 us
    dot_general x11 -> x0, matrix products: 46.2 us -> none  [the longest x3 21.1 us: one_round(): jnp.einsum('qt,tif->qif', selector, products, precision=lax.Precision.HIG...]
    pallas_call x0 -> x1, Pallas kernels: none -> 39.4 us  [per_device_fused(): pl.pallas_call(functools.partial(fused, rows_n, spots), out_shape=jax.Sha...]
    all_gather x1 -> x0, waiting for transfers between devices: 32.8 us -> none  [per_device(): table = lax.all_gather(features, 'blk', axis=0, tiled=True)]
    reduce_scatter x1 -> x0, waiting for transfers between devices: 14 us -> none  [per_device(): lax.psum_scatter(totals.astype(jnp.bfloat16), 'row', scatter_dimension=0,...]
    unnamed x1 -> x0, blocking collectives: 10.1 us -> none
    while x1 -> x0, local copies, waits for them, and re-layouts: 2.08 us -> none  [accumulate(): return lax.fori_loop(0, rounds, one_round, empty)]
    reduce_sum x1 -> x0, other arithmetic: 1.89 us -> none  [per_device(): row_sums = jnp.sum(tiles_here, axis=2, dtype=jnp.float32)]
    unnamed x14 -> x13, local copies, waits for them, and re-layouts: 4.71 us -> 6.27 us
  transfers between devices with their start and end apart: 2 -> 0, of which waited for: 2 -> 0; matrix products, arithmetic and copies ran while one was open for 2% -> 0% of each run, Pallas kernels for 0% -> 0%
where the time goes in v1:
time: 46.6 us; the launch traced here: 46.3 us
  Pallas kernels  39.4 us (85%)
  local copies, waits for them, and re-layouts  6.27 us (13%)
  between operations  0.67 us (1%)
    pallas_call x1, Pallas kernels, per_device_fused(): pl.pallas_call(functools.partial(fused, rows_n, spots), out_shape=jax.Sha...  39.4 us
    unnamed x13, local copies, waits for them, and re-layouts  6.27 us

profile of v1, /device:TPU:0, one launch (start us, length us, event | category | flops | bytes accessed | tf_op | source)
XLA Modules:
  0.0 46.3 jit_solution(16783307774429555622)
XLA Ops:
  0.7 0.0 copy-start
  0.7 1.4 %copy-done = bf16[1,1,48,128,128]{4,3,2,1,0:T(8,128)(2,1)S(1)} copy-done((bf16[1,1,48,128,128]{4,3,2,1,0:T(8,128)(2,1)S(1)}, bf16[1,1,48,128,128]{4,3,2,1,0:T(8,128)(2,1)}, u32[]{:S(2)}) %copy-start) | copy-done | bytes 1572888
  2.1 0.0 copy-start.1
  2.1 1.2 %copy-done.1 = bf16[1024,512]{1,0:T(8,128)(2,1)S(1)} copy-done((bf16[1024,512]{1,0:T(8,128)(2,1)S(1)}, bf16[1024,512]{1,0:T(8,128)(2,1)}, u32[]{:S(2)}) %copy-start.1) | copy-done | bytes 1048600
  3.3 0.0 copy-start.2
  3.3 0.9 %copy-done.2 = bf16[256,512]{1,0:T(8,128)(2,1)S(1)} copy-done((bf16[256,512]{1,0:T(8,128)(2,1)S(1)}, bf16[256,512]{1,0:T(8,128)(2,1)}, u32[]{:S(2)}) %copy-start.2) | copy-done | bytes 262168
  4.2 0.0 copy-start.3
  4.2 0.7 %copy-done.3 = f32[512]{0:T(512)S(1)} copy-done((f32[512]{0:T(512)S(1)}, f32[512]{0:T(512)}, u32[]{:S(2)}) %copy-start.3) | copy-done | bytes 2072
  4.9 0.0 copy-start.4
  4.9 0.7 %copy-done.4 = s32[1,1,48]{2,1,0:T(1,128)S(1)} copy-done((s32[1,1,48]{2,1,0:T(1,128)S(1)}, s32[1,1,48]{2,1,0:T(1,128)}, u32[]{:S(2)}) %copy-start.4) | copy-done | bytes 216
  5.6 0.0 copy-start.5
  5.6 0.7 %copy-done.5 = s32[1,1,48]{2,1,0:T(1,128)S(1)} copy-done((s32[1,1,48]{2,1,0:T(1,128)S(1)}, s32[1,1,48]{2,1,0:T(1,128)}, u32[]{:S(2)}) %copy-start.5) | copy-done | bytes 216
  6.2 39.4 %shard_map.73 = bf16[256,512]{1,0:T(8,128)(2,1)S(1)} custom-call(s32[1,1]{1,0:T(1,128)S(6)} %copy.9.live_ref, s32[1,48]{1,0:T(1,128)S(1)} %bitcast.6, s32[1,48]{1,0:T(1,128)S(1)} %bitcast.7, bf16[256,512]{1,0:T(8,128)(2,1)S(1)} %copy-done.2, bf16[48,128,128]{2,1,0:T(8,128)(2,1)S(1)} %bitcast.4, bf16[1024,512]{1,0:T(8,128)(2,1)S(1)} %copy-done.1, ...), custom_call_target="tpu_custom_call" | custom-call | tf_op jit(solution)/shard_map/pallas_call | solution.py:344
  45.6 0.7 %copy.10 = bf16[256,512]{1,0:T(8,128)(2,1)} copy(bf16[256,512]{1,0:T(8,128)(2,1)S(1)} %shard_map.73) | data formatting | bytes 524288
Async XLA Ops:
  0.7 1.4 %copy-start = (bf16[1,1,48,128,128]{4,3,2,1,0:T(8,128)(2,1)S(1)}, bf16[1,1,48,128,128]{4,3,2,1,0:T(8,128)(2,1)}, u32[]{:S(2)}) copy-start(bf16[1,1,48,128,128]{4,3,2,1,0:T(8,128)(2,1)} %param.8) | copy-start | bytes 4718596
  2.1 1.2 %copy-start.1 = (bf16[1024,512]{1,0:T(8,128)(2,1)S(1)}, bf16[1024,512]{1,0:T(8,128)(2,1)}, u32[]{:S(2)}) copy-start(bf16[1024,512]{1,0:T(8,128)(2,1)} %weight_hbm.1) | copy-start | bytes 3145732
  3.3 0.9 %copy-start.2 = (bf16[256,512]{1,0:T(8,128)(2,1)S(1)}, bf16[256,512]{1,0:T(8,128)(2,1)}, u32[]{:S(2)}) copy-start(bf16[256,512]{1,0:T(8,128)(2,1)} %feat_hbm.1) | copy-start | bytes 786436
  4.2 0.7 %copy-start.3 = (f32[512]{0:T(512)S(1)}, f32[512]{0:T(512)}, u32[]{:S(2)}) copy-start(f32[512]{0:T(512)} %param.13) | copy-start | bytes 6148
  4.9 0.7 %copy-start.4 = (s32[1,1,48]{2,1,0:T(1,128)S(1)}, s32[1,1,48]{2,1,0:T(1,128)}, u32[]{:S(2)}) copy-start(s32[1,1,48]{2,1,0:T(1,128)} %param.9) | copy-start | bytes 580
  5.6 0.7 %copy-start.5 = (s32[1,1,48]{2,1,0:T(1,128)S(1)}, s32[1,1,48]{2,1,0:T(1,128)}, u32[]{:S(2)}) copy-start(s32[1,1,48]{2,1,0:T(1,128)} %param.10) | copy-start | bytes 580

commit v2 on v1

--- a/solution.py
+++ b/solution.py
@@ -14,8 +14,8 @@
 
 
 def fused(
-    rows_n, spots, live_ref, src_ref, dst_ref, feat_hbm, tiles_hbm, weight_hbm, bias_ref, out_ref,
-    tab, tiles, chain, dense, weight, mine, acc, mixed, send_buf, recv_buf, lists, list_smem,
+    rows_n, spots, live_hbm, src_hbm, dst_hbm, feat_hbm, tiles_hbm, weight_hbm, bias_hbm, out_ref,
+    live_ref, src_ref, dst_ref, bias_ref, tab, tiles, chain, dense, weight, mine, acc, mixed, degree, send_buf, recv_buf, lists, list_smem,
     in_sem, own_sem, left_sem, right_sem, side_sem, line_recv, side_recv, row_send, row_recv,
 ):
     slots = tiles.shape[0]
@@ -33,14 +33,6 @@
     c = blk % 2
     side = z * 2 + (1 - c)
 
-    loads = [
-        pltpu.make_async_copy(tiles_hbm, tiles, in_sem.at[0]),
-        pltpu.make_async_copy(feat_hbm, mine, in_sem.at[1]),
-        pltpu.make_async_copy(weight_hbm, weight, in_sem.at[2]),
-    ]
-    for load in loads:
-        load.start()
-
     barrier = pltpu.get_barrier_semaphore()
 
     def greet(r, b):
@@ -113,6 +105,18 @@
 
         side_copy(k, z, True).start()
 
+    loads = [
+        pltpu.make_async_copy(tiles_hbm, tiles, in_sem.at[0]),
+        pltpu.make_async_copy(feat_hbm, mine, in_sem.at[1]),
+        pltpu.make_async_copy(weight_hbm, weight, in_sem.at[2]),
+        pltpu.make_async_copy(bias_hbm, bias_ref, in_sem.at[4]),
+        pltpu.make_async_copy(live_hbm, live_ref, in_sem.at[5]),
+        pltpu.make_async_copy(src_hbm, src_ref, in_sem.at[6]),
+        pltpu.make_async_copy(dst_hbm, dst_ref, in_sem.at[7]),
+    ]
+    for load in loads[4:] + loads[:1]:
+        load.start()
+
     greeted = (
         jnp.where(z > 0, 1, 0) + jnp.where(z < spots - 1, 1, 0) + rows_n
     )
@@ -124,6 +128,10 @@
         return carry
 
     lax.fori_loop(0, min(AHEAD, chunks), first_sends, 0)
+    for load in loads[1:4]:
+        load.start()
+    for load in loads[4:]:
+        load.wait()
 
     list_rows = lists.shape[0] - 1
     lane = lax.broadcasted_iota(jnp.int32, (1, 128), 1)
@@ -134,7 +142,7 @@
 
     def one_key(t, carry):
         keys, last = carry
-        key = dst_ref[0, t] * sources + src_ref[0, t]
+        key = dst_ref[0, 0, t] * sources + src_ref[0, 0, t]
         key = jnp.where(t < live, key, -1)
         return jnp.where(lane == t, key, keys), jnp.where(place == key, t, last)
 
@@ -144,7 +152,7 @@
     )
 
     def one_before(u, before):
-        key = dst_ref[0, u] * sources + src_ref[0, u]
+        key = dst_ref[0, 0, u] * sources + src_ref[0, 0, u]
         key = jnp.where(u < live, key, -2)
         return jnp.where((keys == key) & (lane > u), u, before)
 
@@ -172,7 +180,6 @@
             )
         return carry
 
-    lax.fori_loop(0, dests, one_dest, 0)
 
     def consume(k, p, first):
         block = tab[k, p].reshape(wide * width, CHUNK)
@@ -194,96 +201,95 @@
             total += recv_buf[k, (row + step) % rows_n].astype(jnp.float32)
         return total
 
-    def step_body(s, carry):
-        @pl.when(s + AHEAD < chunks)
-        def _():
-            send_own(s + AHEAD)
-            own_local(s + AHEAD).start()
-
-        for h in range(1, spots):
-            k = s - (h - 1)
-            inside = (k >= 0) & (k < chunks)
-
-            @pl.when(inside & (z + h < spots))
+    def forward(k, h):
+        @pl.when(z + h < spots)
+        def _():
+            line_copy(k, z + h, -1, left_sem, False).wait_recv()
+
+            @pl.when(z > 0)
             def _():
-                line_copy(k, z + h, -1, left_sem, False).wait_recv()
-
-                @pl.when(z > 0)
+                line_copy(k, z + h, -1, left_sem, False).start()
+
+            side_copy(k, z + h, False).start()
+
+        @pl.when(z - h >= 0)
+        def _():
+            line_copy(k, z - h, 1, right_sem, False).wait_recv()
+
+            @pl.when(z < spots - 1)
+            def _():
+                line_copy(k, z - h, 1, right_sem, False).start()
+
+            side_copy(k, z - h, False).start()
+
+    def consume_at(k, h):
+        if h == 0:
+            own_local(k).wait()
+            side_arrival(k, z).wait_recv()
+            consume(k, z, True)
+            return
+
+        @pl.when(z + h < spots)
+        def _():
+            side_arrival(k, z + h).wait_recv()
+            consume(k, z + h, False)
+
+        @pl.when(z - h >= 0)
+        def _():
+            side_arrival(k, z - h).wait_recv()
+            consume(k, z - h, False)
+
+    def finish_mean(k):
+        mean = (gather_rows(k) / degree[...]).astype(jnp.bfloat16)
+        part = weight[pl.ds(pl.multiple_of(feat + k * CHUNK, CHUNK), CHUNK), :]
+        mixed[...] += jnp.dot(mean, part, preferred_element_type=jnp.float32)
+
+    def stage(k, carry):
+        forward(k, 1)
+
+        @pl.when(k + AHEAD < chunks)
+        def _():
+            send_own(k + AHEAD)
+            own_local(k + AHEAD).start()
+
+        @pl.when(k == 0)
+        def _():
+            lax.fori_loop(0, dests, one_dest, 0)
+
+        for h in range(2, spots):
+            forward(k, h)
+            if h == 2:
+                consume_at(k, 0)
+
+                @pl.when(k == 0)
                 def _():
-                    line_copy(k, z + h, -1, left_sem, False).start()
-
-                side_copy(k, z + h, False).start()
-
-            @pl.when(inside & (z - h >= 0))
-            def _():
-                line_copy(k, z - h, 1, right_sem, False).wait_recv()
-
-                @pl.when(z < spots - 1)
-                def _():
-                    line_copy(k, z - h, 1, right_sem, False).start()
-
-                side_copy(k, z - h, False).start()
-
-        @pl.when(s == 0)
-        def _():
-            ones = jnp.ones((wide * width, CHUNK), jnp.bfloat16)
-            total = jnp.dot(dense[0], ones, preferred_element_type=jnp.float32)
-            for p in range(1, spots):
-                total += jnp.dot(dense[p], ones, preferred_element_type=jnp.float32)
-            send_rows(chunks, total)
-
-        @pl.when(s == 1)
-        def _():
-            loads[1].wait()
-            loads[2].wait()
+                    ones = jnp.ones((wide * width, CHUNK), jnp.bfloat16)
+                    total = jnp.dot(dense[0], ones, preferred_element_type=jnp.float32)
+                    for p in range(1, spots):
+                        total += jnp.dot(dense[p], ones, preferred_element_type=jnp.float32)
+                    send_rows(chunks, total)
+
+            consume_at(k, h - 1)
+        consume_at(k, spots - 1)
+        send_rows(k, acc[k])
+
+        @pl.when(k == 0)
+        def _():
+            for load in loads[1:4]:
+                load.wait()
             mixed[...] = (
                 jnp.dot(mine[...], weight[pl.ds(0, feat), :], preferred_element_type=jnp.float32) + bias_ref[...]
             )
-
-        for h in range(spots):
-            k = s - h
-            inside = (k >= 0) & (k < chunks)
-            if h == 0:
-
-                @pl.when(inside)
-                def _():
-                    own_local(k).wait()
-                    side_arrival(k, z).wait_recv()
-                    consume(k, z, True)
-
-            else:
-
-                @pl.when(inside & (z + h < spots))
-                def _():
-                    side_arrival(k, z + h).wait_recv()
-                    consume(k, z + h, False)
-
-                @pl.when(inside & (z - h >= 0))
-                def _():
-                    side_arrival(k, z - h).wait_recv()
-                    consume(k, z - h, False)
-
-        ready = s - (spots - 1)
-
-        @pl.when((ready >= 0) & (ready < chunks))
-        def _():
-            send_rows(ready, acc[ready])
-
-        arrived = s - spots
-
-        @pl.when(arrived == 0)
-        def _():
-            acc[0, pl.ds(0, node_rows), :] = jnp.maximum(gather_rows(chunks), 1.0)
-
-        @pl.when(arrived >= 0)
-        def _():
-            mean = (gather_rows(arrived) / acc[0, pl.ds(0, node_rows), :]).astype(jnp.bfloat16)
-            part = weight[pl.ds(pl.multiple_of(feat + arrived * CHUNK, CHUNK), CHUNK), :]
-            mixed[...] += jnp.dot(mean, part, preferred_element_type=jnp.float32)
-
-        return carry
-
-    lax.fori_loop(0, chunks + spots, step_body, 0)
+            degree[...] = jnp.maximum(gather_rows(chunks), 1.0)
+
+        @pl.when(k > 0)
+        def _():
+            finish_mean(k - 1)
+
+        return carry
+
+    lax.fori_loop(0, chunks, stage, 0)
+    finish_mean(chunks - 1)
     out_ref[...] = jnp.maximum(mixed[...], 0.0).astype(jnp.bfloat16)
 
     def finish(k, carry):
@@ -337,16 +343,19 @@
     dests, sources = rows_n * per_node, spots * 2 * per_node
     list_rows = -(-dests * sources // 128)
     dest_rows = rows_n * node_rows
-    hbm = pl.BlockSpec(memory_space=pl.ANY)
-    smem = pl.BlockSpec(memory_space=pltpu.SMEM)
+    hbm = pl.BlockSpec(memory_space=pltpu.HBM)
     vmem = pl.BlockSpec(memory_space=pltpu.VMEM)
     dma = pltpu.SemaphoreType.DMA
     return pl.pallas_call(
         functools.partial(fused, rows_n, spots),
         out_shape=jax.ShapeDtypeStruct((node_rows, feat), jnp.bfloat16),
-        in_specs=[smem, smem, smem, hbm, hbm, hbm, vmem],
+        in_specs=[hbm] * 7,
         out_specs=vmem,
         scratch_shapes=[
+            pltpu.SMEM(tile_count.shape, jnp.int32),
+            pltpu.SMEM(tile_src.shape, jnp.int32),
+            pltpu.SMEM(tile_dst.shape, jnp.int32),
+            pltpu.VMEM((1, feat), jnp.float32),
             pltpu.VMEM((chunks, spots, 2, node_rows, CHUNK), jnp.bfloat16),
             pltpu.VMEM((slots, width, width), jnp.bfloat16),
             pltpu.VMEM((slots + 1, width, width), jnp.float32),
@@ -355,11 +364,12 @@
             pltpu.VMEM((node_rows, feat), jnp.bfloat16),
             pltpu.VMEM((chunks, dest_rows, CHUNK), jnp.float32),
             pltpu.VMEM((node_rows, feat), jnp.float32),
+            pltpu.VMEM((node_rows, CHUNK), jnp.float32),
             pltpu.VMEM((chunks + 1, rows_n, node_rows, CHUNK), jnp.bfloat16),
             pltpu.VMEM((chunks + 1, rows_n, node_rows, CHUNK), jnp.bfloat16),
             pltpu.VMEM((list_rows + 1, 128), jnp.int32),
             pltpu.SMEM((list_rows + 1, 128), jnp.int32),
-            dma((4,)),
+            dma((8,)),
             dma((chunks,)),
             dma((chunks, spots)),
             dma((chunks, spots)),
@@ -370,12 +380,12 @@
             dma((chunks + 1, rows_n)),
         ],
         compiler_params=pltpu.CompilerParams(
-            collective_id=0, has_side_effects=True, vmem_limit_bytes=48 * 2**20
+            collective_id=0, has_side_effects=True, vmem_limit_bytes=60 * 2**20
         ),
     )(
         tile_count,
-        tile_src.reshape(1, slots),
-        tile_dst.reshape(1, slots),
+        tile_src,
+        tile_dst,
         features,
         edge_tiles.reshape(slots, width, width),
         weight,

time: 46.6 us -> 47.5 us (1.019)
  Pallas kernels: 39.4 us -> 45 us
  local copies, waits for them, and re-layouts: 6.27 us -> 1.67 us
    pallas_call x1, Pallas kernels: 39.4 us -> 45 us  [per_device_fused(): pl.pallas_call(functools.partial(fused, rows_n, spots), out_shape=jax.Sha...]
    unnamed x13 -> x1, local copies, waits for them, and re-layouts: 6.27 us -> 1.67 us
where the time goes in v2:
time: 47.5 us; the launch traced here: 47.4 us
  Pallas kernels  45 us (95%)
  local copies, waits for them, and re-layouts  1.67 us (4%)
  between operations  0.66 us (1%)
    pallas_call x1, Pallas kernels, per_device_fused(): pl.pallas_call(functools.partial(fused, rows_n, spots), out_shape=jax.Sha...  45 us
    unnamed x1, local copies, waits for them, and re-layouts  1.67 us

profile of v2, /device:TPU:0, one launch (start us, length us, event | category | flops | bytes accessed | tf_op | source)
XLA Modules:
  0.0 47.4 jit_solution(9844764146704164783)
XLA Ops:
  0.7 45.0 %shard_map.73 = bf16[256,512]{1,0:T(8,128)(2,1)} custom-call(s32[1,1]{1,0:T(1,128)S(6)} %copy.9.live_hbm, s32[1,1,48]{2,1,0:T(1,128)} %src_hbm.1, s32[1,1,48]{2,1,0:T(1,128)} %dst_hbm.1, bf16[256,512]{1,0:T(8,128)(2,1)} %feat_hbm.1, bf16[48,128,128]{2,1,0:T(8,128)(2,1)} %bitcast.2, bf16[1024,512]{1,0:T(8,128)(2,1)} %weight_hbm.1, f32[1,512]{1,0:T(1,128)} %bitcast.3), custom_call_target="tpu_custom_call" | custom-call | tf_op jit(solution)/shard_map/pallas_call | solution.py:349
  45.7 1.7 %copy.10 = bf16[256,512]{1,0:T(8,128)(2,1)} copy(bf16[256,512]{1,0:T(8,128)(2,1)} %shard_map.73) | data formatting | bytes 524288

commit v3 on v2

--- a/solution.py
+++ b/solution.py
@@ -9,14 +9,14 @@
 
 MESH = pl.DeviceIdType.MESH
 CHUNK = 128
-AHEAD = 3
+AHEAD = 2
 DENSE_LIMIT = 12 * 2**20
 
 
 def fused(
     rows_n, spots, live_hbm, src_hbm, dst_hbm, feat_hbm, tiles_hbm, weight_hbm, bias_hbm, out_ref,
     live_ref, src_ref, dst_ref, bias_ref, tab, tiles, chain, dense, weight, mine, acc, mixed, degree, send_buf, recv_buf, lists, list_smem,
-    in_sem, own_sem, left_sem, right_sem, side_sem, line_recv, side_recv, row_send, row_recv,
+    in_sem, own_sem, left_sem, right_sem, far_left_sem, far_right_sem, side_sem, line_recv, side_recv, row_send, row_recv,
 ):
     slots = tiles.shape[0]
     width = tiles.shape[-1]
@@ -46,6 +46,14 @@
     def _():
         greet(row, blk + 2)
 
+    @pl.when(z > 1)
+    def _():
+        greet(row, blk - 4)
+
+    @pl.when(z < spots - 2)
+    def _():
+        greet(row, blk + 4)
+
     greet(row, side)
     for step in range(1, rows_n):
         greet((row + step) % rows_n, blk)
@@ -55,19 +63,24 @@
             feat_hbm.at[:, pl.ds(pl.multiple_of(k * CHUNK, CHUNK), CHUNK)], tab.at[k, z, c], own_sem.at[k]
         )
 
-    def line_copy(k, p, step, sems, own):
+    def line_copy(k, p, step, sems):
         slot = tab.at[k, p, c]
-        source = feat_hbm.at[:, pl.ds(pl.multiple_of(k * CHUNK, CHUNK), CHUNK)] if own else slot
         return pltpu.make_async_remote_copy(
-            src_ref=source, dst_ref=slot, send_sem=sems.at[k, p], recv_sem=line_recv.at[k, p],
+            src_ref=slot, dst_ref=slot, send_sem=sems.at[k, p], recv_sem=line_recv.at[k, p],
             device_id=(row, blk + 2 * step), device_id_type=MESH,
         )
 
-    def side_copy(k, p, own):
+    def far_copy(k, step, sems):
+        slot = tab.at[k, z, c]
+        return pltpu.make_async_remote_copy(
+            src_ref=slot, dst_ref=slot, send_sem=sems.at[k], recv_sem=line_recv.at[k, z],
+            device_id=(row, blk + 4 * step), device_id_type=MESH,
+        )
+
+    def side_copy(k, p):
         slot = tab.at[k, p, c]
-        source = feat_hbm.at[:, pl.ds(pl.multiple_of(k * CHUNK, CHUNK), CHUNK)] if own else slot
         return pltpu.make_async_remote_copy(
-            src_ref=source, dst_ref=slot, send_sem=side_sem.at[k, p], recv_sem=side_recv.at[k, p],
+            src_ref=slot, dst_ref=slot, send_sem=side_sem.at[k, p], recv_sem=side_recv.at[k, p],
             device_id=(row, side), device_id_type=MESH,
         )
 
@@ -95,15 +108,25 @@
         )
 
     def send_own(k):
+        own_local(k).wait()
+
         @pl.when(z > 0)
         def _():
-            line_copy(k, z, -1, left_sem, True).start()
+            line_copy(k, z, -1, left_sem).start()
 
         @pl.when(z < spots - 1)
         def _():
-            line_copy(k, z, 1, right_sem, True).start()
-
-        side_copy(k, z, True).start()
+            line_copy(k, z, 1, right_sem).start()
+
+        @pl.when(z > 1)
+        def _():
+            far_copy(k, -1, far_left_sem).start()
+
+        @pl.when(z < spots - 2)
+        def _():
+            far_copy(k, 1, far_right_sem).start()
+
+        side_copy(k, z).start()
 
     loads = [
         pltpu.make_async_copy(tiles_hbm, tiles, in_sem.at[0]),
@@ -114,17 +137,20 @@
         pltpu.make_async_copy(src_hbm, src_ref, in_sem.at[6]),
         pltpu.make_async_copy(dst_hbm, dst_ref, in_sem.at[7]),
     ]
-    for load in loads[4:] + loads[:1]:
+    for load in loads[4:]:
         load.start()
+    for k in range(chunks):
+        own_local(k).start()
+    loads[0].start()
 
     greeted = (
         jnp.where(z > 0, 1, 0) + jnp.where(z < spots - 1, 1, 0) + rows_n
+        + jnp.where(z > 1, 1, 0) + jnp.where(z < spots - 2, 1, 0)
     )
     pl.semaphore_wait(barrier, greeted)
 
     def first_sends(k, carry):
         send_own(k)
-        own_local(k).start()
         return carry
 
     lax.fori_loop(0, min(AHEAD, chunks), first_sends, 0)
@@ -172,13 +198,21 @@
     lax.fori_loop(0, slots, one_link, 0, unroll=4)
 
     def one_dest(q, carry):
+        total = jnp.zeros((width, width), jnp.float32)
         for s in range(sources):
             at = q * sources + s
             block = chain[list_smem[at // 128, at % 128]]
             dense[s // wide, pl.ds(pl.multiple_of(q * width, width), width), pl.ds(s % wide * width, width)] = (
                 block.astype(jnp.bfloat16)
             )
+            total += block
+        degrees = jnp.broadcast_to(jnp.sum(total, axis=1, keepdims=True), (width, CHUNK))
+        send_buf[chunks, q // per_node, pl.ds(pl.multiple_of(q % per_node * width, width), width), :] = (
+            degrees.astype(jnp.bfloat16)
+        )
         return carry
+
+    lax.fori_loop(0, dests, one_dest, 0)
 
 
     def consume(k, p, first):
@@ -189,8 +223,7 @@
         else:
             acc[k] += product
 
-    def send_rows(k, values):
-        send_buf[k] = values.astype(jnp.bfloat16).reshape(rows_n, node_rows, CHUNK)
+    def send_rows(k):
         for step in range(1, rows_n):
             row_copy(k, step).start()
 
@@ -204,27 +237,28 @@
     def forward(k, h):
         @pl.when(z + h < spots)
         def _():
-            line_copy(k, z + h, -1, left_sem, False).wait_recv()
-
-            @pl.when(z > 0)
-            def _():
-                line_copy(k, z + h, -1, left_sem, False).start()
-
-            side_copy(k, z + h, False).start()
+            line_copy(k, z + h, -1, left_sem).wait_recv()
+            if h > 1:
+
+                @pl.when(z > 0)
+                def _():
+                    line_copy(k, z + h, -1, left_sem).start()
+
+            side_copy(k, z + h).start()
 
         @pl.when(z - h >= 0)
         def _():
-            line_copy(k, z - h, 1, right_sem, False).wait_recv()
-
-            @pl.when(z < spots - 1)
-            def _():
-                line_copy(k, z - h, 1, right_sem, False).start()
-
-            side_copy(k, z - h, False).start()
+            line_copy(k, z - h, 1, right_sem).wait_recv()
+            if h > 1:
+
+                @pl.when(z < spots - 1)
+                def _():
+                    line_copy(k, z - h, 1, right_sem).start()
+
+            side_copy(k, z - h).start()
 
     def consume_at(k, h):
         if h == 0:
-            own_local(k).wait()
             side_arrival(k, z).wait_recv()
             consume(k, z, True)
             return
@@ -244,34 +278,22 @@
         part = weight[pl.ds(pl.multiple_of(feat + k * CHUNK, CHUNK), CHUNK), :]
         mixed[...] += jnp.dot(mean, part, preferred_element_type=jnp.float32)
 
+    send_rows(chunks)
+
     def stage(k, carry):
-        forward(k, 1)
+        for h in range(1, min(3, spots)):
+            forward(k, h)
 
         @pl.when(k + AHEAD < chunks)
         def _():
             send_own(k + AHEAD)
-            own_local(k + AHEAD).start()
-
-        @pl.when(k == 0)
-        def _():
-            lax.fori_loop(0, dests, one_dest, 0)
-
-        for h in range(2, spots):
-            forward(k, h)
-            if h == 2:
-                consume_at(k, 0)
-
-                @pl.when(k == 0)
-                def _():
-                    ones = jnp.ones((wide * width, CHUNK), jnp.bfloat16)
-                    total = jnp.dot(dense[0], ones, preferred_element_type=jnp.float32)
-                    for p in range(1, spots):
-                        total += jnp.dot(dense[p], ones, preferred_element_type=jnp.float32)
-                    send_rows(chunks, total)
-
-            consume_at(k, h - 1)
-        consume_at(k, spots - 1)
-        send_rows(k, acc[k])
+
+        for h in range(spots):
+            if h > 2:
+                forward(k, h)
+            consume_at(k, h)
+        send_buf[k] = acc[k].astype(jnp.bfloat16).reshape(rows_n, node_rows, CHUNK)
+        send_rows(k)
 
         @pl.when(k == 0)
         def _():
@@ -293,33 +315,43 @@
     out_ref[...] = jnp.maximum(mixed[...], 0.0).astype(jnp.bfloat16)
 
     def finish(k, carry):
-        side_copy(k, z, True).wait_send()
+        side_copy(k, z).wait_send()
 
         @pl.when(z > 0)
         def _():
-            line_copy(k, z, -1, left_sem, True).wait_send()
+            line_copy(k, z, -1, left_sem).wait_send()
 
         @pl.when(z < spots - 1)
         def _():
-            line_copy(k, z, 1, right_sem, True).wait_send()
+            line_copy(k, z, 1, right_sem).wait_send()
+
+        @pl.when(z > 1)
+        def _():
+            far_copy(k, -1, far_left_sem).wait_send()
+
+        @pl.when(z < spots - 2)
+        def _():
+            far_copy(k, 1, far_right_sem).wait_send()
 
         for h in range(1, spots):
 
             @pl.when(z + h < spots)
             def _():
-                side_copy(k, z + h, False).wait_send()
-
-                @pl.when(z > 0)
-                def _():
-                    line_copy(k, z + h, -1, left_sem, False).wait_send()
+                side_copy(k, z + h).wait_send()
+                if h > 1:
+
+                    @pl.when(z > 0)
+                    def _():
+                        line_copy(k, z + h, -1, left_sem).wait_send()
 
             @pl.when(z - h >= 0)
             def _():
-                side_copy(k, z - h, False).wait_send()
-
-                @pl.when(z < spots - 1)
-                def _():
-                    line_copy(k, z - h, 1, right_sem, False).wait_send()
+                side_copy(k, z - h).wait_send()
+                if h > 1:
+
+                    @pl.when(z < spots - 1)
+                    def _():
+                        line_copy(k, z - h, 1, right_sem).wait_send()
 
         return carry
 
@@ -373,6 +405,8 @@
             dma((chunks,)),
             dma((chunks, spots)),
             dma((chunks, spots)),
+            dma((chunks,)),
+            dma((chunks,)),
             dma((chunks, spots)),
             dma((chunks, spots)),
             dma((chunks, spots)),
@@ -380,7 +414,7 @@
             dma((chunks + 1, rows_n)),
         ],
         compiler_params=pltpu.CompilerParams(
-            collective_id=0, has_side_effects=True, vmem_limit_bytes=60 * 2**20
+            collective_id=0, has_side_effects=True, vmem_limit_bytes=56 * 2**20
         ),
     )(
         tile_count,

time: 47.5 us -> 38.8 us (0.82)
  Pallas kernels: 45 us -> 36.3 us
    pallas_call x1, Pallas kernels: 45 us -> 36.3 us  [per_device_fused(): pl.pallas_call(functools.partial(fused, rows_n, spots), out_shape=jax.Sha...]
where the time goes in v3:
time: 38.8 us; the launch traced here: 38.6 us
  Pallas kernels  36.3 us (94%)
  local copies, waits for them, and re-layouts  1.67 us (4%)
  between operations  0.66 us (2%)
    pallas_call x1, Pallas kernels, per_device_fused(): pl.pallas_call(functools.partial(fused, rows_n, spots), out_shape=jax.Sha...  36.3 us
    unnamed x1, local copies, waits for them, and re-layouts  1.67 us

profile of v3, /device:TPU:0, one launch (start us, length us, event | category | flops | bytes accessed | tf_op | source)
XLA Modules:
  0.0 38.6 jit_solution(5418959856232622022)
XLA Ops:
  0.7 36.3 %shard_map.73 = bf16[256,512]{1,0:T(8,128)(2,1)} custom-call(s32[1,1]{1,0:T(1,128)S(6)} %copy.9.live_hbm, s32[1,1,48]{2,1,0:T(1,128)} %src_hbm.1, s32[1,1,48]{2,1,0:T(1,128)} %dst_hbm.1, bf16[256,512]{1,0:T(8,128)(2,1)} %feat_hbm.1, bf16[48,128,128]{2,1,0:T(8,128)(2,1)} %bitcast.2, bf16[1024,512]{1,0:T(8,128)(2,1)} %weight_hbm.1, f32[1,512]{1,0:T(1,128)} %bitcast.3), custom_call_target="tpu_custom_call" | custom-call | tf_op jit(solution)/shard_map/pallas_call | solution.py:381
  37.0 1.7 %copy.10 = bf16[256,512]{1,0:T(8,128)(2,1)} copy(bf16[256,512]{1,0:T(8,128)(2,1)} %shard_map.73) | data formatting | bytes 524288

commit v4 on v3

--- a/solution.py
+++ b/solution.py
@@ -10,6 +10,7 @@
 MESH = pl.DeviceIdType.MESH
 CHUNK = 128
 AHEAD = 2
+FAR = 2
 DENSE_LIMIT = 12 * 2**20
 
 
@@ -118,11 +119,11 @@
         def _():
             line_copy(k, z, 1, right_sem).start()
 
-        @pl.when(z > 1)
+        @pl.when((z > 1) & (k < FAR))
         def _():
             far_copy(k, -1, far_left_sem).start()
 
-        @pl.when(z < spots - 2)
+        @pl.when((z < spots - 2) & (k < FAR))
         def _():
             far_copy(k, 1, far_right_sem).start()
 
@@ -234,26 +235,27 @@
             total += recv_buf[k, (row + step) % rows_n].astype(jnp.float32)
         return total
 
+    def handed(k, h):
+        return (k >= FAR) | (h > 1)
+
     def forward(k, h):
         @pl.when(z + h < spots)
         def _():
             line_copy(k, z + h, -1, left_sem).wait_recv()
-            if h > 1:
-
-                @pl.when(z > 0)
-                def _():
-                    line_copy(k, z + h, -1, left_sem).start()
+
+            @pl.when((z > 0) & handed(k, h))
+            def _():
+                line_copy(k, z + h, -1, left_sem).start()
 
             side_copy(k, z + h).start()
 
         @pl.when(z - h >= 0)
         def _():
             line_copy(k, z - h, 1, right_sem).wait_recv()
-            if h > 1:
-
-                @pl.when(z < spots - 1)
-                def _():
-                    line_copy(k, z - h, 1, right_sem).start()
+
+            @pl.when((z < spots - 1) & handed(k, h))
+            def _():
+                line_copy(k, z - h, 1, right_sem).start()
 
             side_copy(k, z - h).start()
 
@@ -279,14 +281,24 @@
         mixed[...] += jnp.dot(mean, part, preferred_element_type=jnp.float32)
 
     send_rows(chunks)
+    inner = (z > 0) & (z < spots - 1)
+
+    def pass_on(k):
+        forward(k, 1)
+
+        @pl.when(k + AHEAD < chunks)
+        def _():
+            send_own(k + AHEAD)
+
+        for h in range(2, min(3, spots)):
+            forward(k, h)
+
+    pass_on(0)
 
     def stage(k, carry):
-        for h in range(1, min(3, spots)):
-            forward(k, h)
-
-        @pl.when(k + AHEAD < chunks)
-        def _():
-            send_own(k + AHEAD)
+        @pl.when(inner & (k + 1 < chunks))
+        def _():
+            pass_on(k + 1)
 
         for h in range(spots):
             if h > 2:
@@ -295,6 +307,10 @@
         send_buf[k] = acc[k].astype(jnp.bfloat16).reshape(rows_n, node_rows, CHUNK)
         send_rows(k)
 
+        @pl.when(jnp.logical_not(inner) & (k + 1 < chunks))
+        def _():
+            pass_on(k + 1)
+
         @pl.when(k == 0)
         def _():
             for load in loads[1:4]:
@@ -312,7 +328,7 @@
 
     lax.fori_loop(0, chunks, stage, 0)
     finish_mean(chunks - 1)
-    out_ref[...] = jnp.maximum(mixed[...], 0.0).astype(jnp.bfloat16)
+    out_ref[...] = mixed[...].astype(jnp.bfloat16)
 
     def finish(k, carry):
         side_copy(k, z).wait_send()
@@ -325,11 +341,11 @@
         def _():
             line_copy(k, z, 1, right_sem).wait_send()
 
-        @pl.when(z > 1)
+        @pl.when((z > 1) & (k < FAR))
         def _():
             far_copy(k, -1, far_left_sem).wait_send()
 
-        @pl.when(z < spots - 2)
+        @pl.when((z < spots - 2) & (k < FAR))
         def _():
             far_copy(k, 1, far_right_sem).wait_send()
 
@@ -338,20 +354,18 @@
             @pl.when(z + h < spots)
             def _():
                 side_copy(k, z + h).wait_send()
-                if h > 1:
-
-                    @pl.when(z > 0)
-                    def _():
-                        line_copy(k, z + h, -1, left_sem).wait_send()
+
+                @pl.when((z > 0) & handed(k, h))
+                def _():
+                    line_copy(k, z + h, -1, left_sem).wait_send()
 
             @pl.when(z - h >= 0)
             def _():
                 side_copy(k, z - h).wait_send()
-                if h > 1:
-
-                    @pl.when(z < spots - 1)
-                    def _():
-                        line_copy(k, z - h, 1, right_sem).wait_send()
+
+                @pl.when((z < spots - 1) & handed(k, h))
+                def _():
+                    line_copy(k, z - h, 1, right_sem).wait_send()
 
         return carry
 
@@ -378,7 +392,7 @@
     hbm = pl.BlockSpec(memory_space=pltpu.HBM)
     vmem = pl.BlockSpec(memory_space=pltpu.VMEM)
     dma = pltpu.SemaphoreType.DMA
-    return pl.pallas_call(
+    mixed = pl.pallas_call(
         functools.partial(fused, rows_n, spots),
         out_shape=jax.ShapeDtypeStruct((node_rows, feat), jnp.bfloat16),
         in_specs=[hbm] * 7,
@@ -425,6 +439,7 @@
         weight,
         out_bias.reshape(1, feat),
     )
+    return jax.nn.relu(mixed)
 
 
 def accumulate(table, block_of, tiles_here, target_ids, live_slot, dest_blocks):

time: 38.8 us -> 39.2 us (1.010)
  other arithmetic: 0 us -> 1.67 us
  local copies, waits for them, and re-layouts: 1.67 us -> 0 us
  Pallas kernels: 36.3 us -> 36.8 us
    max x0 -> x1, other arithmetic: none -> 1.67 us  [per_device_fused(): return jax.nn.relu(mixed)]
    unnamed x1 -> x0, local copies, waits for them, and re-layouts: 1.67 us -> none
    pallas_call x1, Pallas kernels: 36.3 us -> 36.8 us  [per_device_fused(): pl.pallas_call(functools.partial(fused, rows_n, spots), out_shape=jax.Sha...]
where the time goes in v4:
time: 39.2 us; the launch traced here: 39.1 us
  Pallas kernels  36.8 us (94%)
  other arithmetic  1.67 us (4%)
  between operations  0.66 us (2%)
    pallas_call x1, Pallas kernels, per_device_fused(): pl.pallas_call(functools.partial(fused, rows_n, spots), out_shape=jax.Sha...  36.8 us
    max x1, other arithmetic, per_device_fused(): return jax.nn.relu(mixed)  1.67 us

profile of v4, /device:TPU:0, one launch (start us, length us, event | category | flops | bytes accessed | tf_op | source)
XLA Modules:
  0.0 39.1 jit_solution(7126768563952403120)
XLA Ops:
  0.7 36.8 %shard_map.73 = bf16[256,512]{1,0:T(8,128)(2,1)} custom-call(s32[1,1]{1,0:T(1,128)S(6)} %copy.8.live_hbm, s32[1,1,48]{2,1,0:T(1,128)} %src_hbm.1, s32[1,1,48]{2,1,0:T(1,128)} %dst_hbm.1, bf16[256,512]{1,0:T(8,128)(2,1)} %feat_hbm.1, bf16[48,128,128]{2,1,0:T(8,128)(2,1)} %bitcast.2, bf16[1024,512]{1,0:T(8,128)(2,1)} %weight_hbm.1, f32[1,512]{1,0:T(1,128)} %bitcast.3), custom_call_target="tpu_custom_call" | custom-call | tf_op jit(solution)/shard_map/pallas_call | solution.py:395
  37.4 1.7 %broadcast_maximum_fusion = bf16[256,512]{1,0:T(8,128)(2,1)} fusion(bf16[256,512]{1,0:T(8,128)(2,1)} %shard_map.73), kind=kLoop, calls=%fused_computation | loop fusion | flops 131072 | bytes 524288 | tf_op jit(solution)/shard_map/jit(relu)/max | solution.py:442

commit v5 on v4

--- a/solution.py
+++ b/solution.py
@@ -9,8 +9,8 @@
 
 MESH = pl.DeviceIdType.MESH
 CHUNK = 128
-AHEAD = 2
-FAR = 2
+AHEAD = 3
+FAR = 4
 DENSE_LIMIT = 12 * 2**20
 
 
@@ -213,8 +213,6 @@
         )
         return carry
 
-    lax.fori_loop(0, dests, one_dest, 0)
-
 
     def consume(k, p, first):
         block = tab[k, p].reshape(wide * width, CHUNK)
@@ -259,6 +257,17 @@
 
             side_copy(k, z - h).start()
 
+    def near(k):
+        forward(k, 1)
+
+        @pl.when(k + AHEAD < chunks)
+        def _():
+            send_own(k + AHEAD)
+
+    def far(k):
+        if spots > 2:
+            forward(k, 2)
+
     def consume_at(k, h):
         if h == 0:
             side_arrival(k, z).wait_recv()
@@ -280,36 +289,21 @@
         part = weight[pl.ds(pl.multiple_of(feat + k * CHUNK, CHUNK), CHUNK), :]
         mixed[...] += jnp.dot(mean, part, preferred_element_type=jnp.float32)
 
+    near(0)
+    lax.fori_loop(0, dests, one_dest, 0)
     send_rows(chunks)
-    inner = (z > 0) & (z < spots - 1)
-
-    def pass_on(k):
-        forward(k, 1)
-
-        @pl.when(k + AHEAD < chunks)
-        def _():
-            send_own(k + AHEAD)
-
-        for h in range(2, min(3, spots)):
-            forward(k, h)
-
-    pass_on(0)
-
     def stage(k, carry):
-        @pl.when(inner & (k + 1 < chunks))
-        def _():
-            pass_on(k + 1)
-
+        @pl.when(k > 0)
+        def _():
+            near(k)
+
+        far(k)
         for h in range(spots):
             if h > 2:
                 forward(k, h)
             consume_at(k, h)
         send_buf[k] = acc[k].astype(jnp.bfloat16).reshape(rows_n, node_rows, CHUNK)
         send_rows(k)
-
-        @pl.when(jnp.logical_not(inner) & (k + 1 < chunks))
-        def _():
-            pass_on(k + 1)
 
         @pl.when(k == 0)
         def _():

time: 39.2 us -> 40.5 us (1.033)
  Pallas kernels: 36.8 us -> 38 us
    pallas_call x1, Pallas kernels: 36.8 us -> 38 us  [per_device_fused(): pl.pallas_call(functools.partial(fused, rows_n, spots), out_shape=jax.Sha...]
where the time goes in v5:
time: 40.5 us; the launch traced here: 40.3 us
  Pallas kernels  38 us (94%)
  other arithmetic  1.67 us (4%)
  between operations  0.66 us (2%)
    pallas_call x1, Pallas kernels, per_device_fused(): pl.pallas_call(functools.partial(fused, rows_n, spots), out_shape=jax.Sha...  38 us
    max x1, other arithmetic, per_device_fused(): return jax.nn.relu(mixed)  1.67 us

profile of v5, /device:TPU:0, one launch (start us, length us, event | category | flops | bytes accessed | tf_op | source)
XLA Modules:
  0.0 40.3 jit_solution(2474948847935192032)
XLA Ops:
  0.7 38.0 %shard_map.73 = bf16[256,512]{1,0:T(8,128)(2,1)} custom-call(s32[1,1]{1,0:T(1,128)S(6)} %copy.8.live_hbm, s32[1,1,48]{2,1,0:T(1,128)} %src_hbm.1, s32[1,1,48]{2,1,0:T(1,128)} %dst_hbm.1, bf16[256,512]{1,0:T(8,128)(2,1)} %feat_hbm.1, bf16[48,128,128]{2,1,0:T(8,128)(2,1)} %bitcast.2, bf16[1024,512]{1,0:T(8,128)(2,1)} %weight_hbm.1, f32[1,512]{1,0:T(1,128)} %bitcast.3), custom_call_target="tpu_custom_call" | custom-call | tf_op jit(solution)/shard_map/pallas_call | solution.py:389
  38.7 1.7 %broadcast_maximum_fusion = bf16[256,512]{1,0:T(8,128)(2,1)} fusion(bf16[256,512]{1,0:T(8,128)(2,1)} %shard_map.73), kind=kLoop, calls=%fused_computation | loop fusion | flops 131072 | bytes 524288 | tf_op jit(solution)/shard_map/jit(relu)/max | solution.py:436

commit v6 on v3

--- a/solution.py
+++ b/solution.py
@@ -8,7 +8,7 @@
 from jax.sharding import PartitionSpec as P
 
 MESH = pl.DeviceIdType.MESH
-CHUNK = 128
+CHUNK = 256
 AHEAD = 2
 DENSE_LIMIT = 12 * 2**20
 

time: 38.8 us -> 39.5 us (1.018)
  Pallas kernels: 36.3 us -> 37.1 us
    pallas_call x1, Pallas kernels: 36.3 us -> 37.1 us  [per_device_fused(): pl.pallas_call(functools.partial(fused, rows_n, spots), out_shape=jax.Sha...]
where the time goes in v6:
time: 39.5 us; the launch traced here: 39.4 us
  Pallas kernels  37.1 us (94%)
  local copies, waits for them, and re-layouts  1.67 us (4%)
  between operations  0.66 us (2%)
    pallas_call x1, Pallas kernels, per_device_fused(): pl.pallas_call(functools.partial(fused, rows_n, spots), out_shape=jax.Sha...  37.1 us
    unnamed x1, local copies, waits for them, and re-layouts  1.67 us

profile of v6, /device:TPU:0, one launch (start us, length us, event | category | flops | bytes accessed | tf_op | source)
XLA Modules:
  0.0 39.4 jit_solution(4187211086498504651)
XLA Ops:
  0.7 37.1 %shard_map.73 = bf16[256,512]{1,0:T(8,128)(2,1)} custom-call(s32[1,1]{1,0:T(1,128)S(6)} %copy.9.live_hbm, s32[1,1,48]{2,1,0:T(1,128)} %src_hbm.1, s32[1,1,48]{2,1,0:T(1,128)} %dst_hbm.1, bf16[256,512]{1,0:T(8,128)(2,1)} %feat_hbm.1, bf16[48,128,128]{2,1,0:T(8,128)(2,1)} %bitcast.2, bf16[1024,512]{1,0:T(8,128)(2,1)} %weight_hbm.1, f32[1,512]{1,0:T(1,128)} %bitcast.3), custom_call_target="tpu_custom_call" | custom-call | tf_op jit(solution)/shard_map/pallas_call | solution.py:381
  37.7 1.7 %copy.10 = bf16[256,512]{1,0:T(8,128)(2,1)} copy(bf16[256,512]{1,0:T(8,128)(2,1)} %shard_map.73) | data formatting | bytes 524288

commit v7 on v3

--- a/solution.py
+++ b/solution.py
@@ -110,6 +110,14 @@
     def send_own(k):
         own_local(k).wait()
 
+        @pl.when(z > 1)
+        def _():
+            far_copy(k, -1, far_left_sem).start()
+
+        @pl.when(z < spots - 2)
+        def _():
+            far_copy(k, 1, far_right_sem).start()
+
         @pl.when(z > 0)
         def _():
             line_copy(k, z, -1, left_sem).start()
@@ -117,14 +125,6 @@
         @pl.when(z < spots - 1)
         def _():
             line_copy(k, z, 1, right_sem).start()
-
-        @pl.when(z > 1)
-        def _():
-            far_copy(k, -1, far_left_sem).start()
-
-        @pl.when(z < spots - 2)
-        def _():
-            far_copy(k, 1, far_right_sem).start()
 
         side_copy(k, z).start()
 
@@ -149,11 +149,13 @@
     )
     pl.semaphore_wait(barrier, greeted)
 
+    inner = (z > 0) & (z < spots - 1)
+
     def first_sends(k, carry):
         send_own(k)
         return carry
 
-    lax.fori_loop(0, min(AHEAD, chunks), first_sends, 0)
+    lax.fori_loop(0, jnp.where(inner, min(AHEAD, chunks), chunks), first_sends, 0)
     for load in loads[1:4]:
         load.start()
     for load in loads[4:]:
@@ -281,12 +283,24 @@
     send_rows(chunks)
 
     def stage(k, carry):
-        for h in range(1, min(3, spots)):
-            forward(k, h)
-
-        @pl.when(k + AHEAD < chunks)
+        forward(k, 1)
+
+        @pl.when(inner & (k + AHEAD < chunks))
         def _():
             send_own(k + AHEAD)
+
+        if spots > 2:
+            @pl.when(inner & (k == 0))
+            def _():
+                forward(k, 2)
+
+            @pl.when(inner & (k + 1 < chunks))
+            def _():
+                forward(k + 1, 2)
+
+            @pl.when(jnp.logical_not(inner))
+            def _():
+                forward(k, 2)
 
         for h in range(spots):
             if h > 2:

time: 38.8 us -> 42.3 us (1.090)
  Pallas kernels: 36.3 us -> 39.8 us
    pallas_call x1, Pallas kernels: 36.3 us -> 39.8 us  [per_device_fused(): pl.pallas_call(functools.partial(fused, rows_n, spots), out_shape=jax.Sha...]
where the time goes in v7:
time: 42.3 us; the launch traced here: 42.1 us
  Pallas kernels  39.8 us (94%)
  local copies, waits for them, and re-layouts  1.67 us (4%)
  between operations  0.66 us (2%)
    pallas_call x1, Pallas kernels, per_device_fused(): pl.pallas_call(functools.partial(fused, rows_n, spots), out_shape=jax.Sha...  39.8 us
    unnamed x1, local copies, waits for them, and re-layouts  1.67 us

profile of v7, /device:TPU:0, one launch (start us, length us, event | category | flops | bytes accessed | tf_op | source)
XLA Modules:
  0.0 42.1 jit_solution(12521685066644198660)
XLA Ops:
  0.7 39.8 %shard_map.73 = bf16[256,512]{1,0:T(8,128)(2,1)} custom-call(s32[1,1]{1,0:T(1,128)S(6)} %copy.9.live_hbm, s32[1,1,48]{2,1,0:T(1,128)} %src_hbm.1, s32[1,1,48]{2,1,0:T(1,128)} %dst_hbm.1, bf16[256,512]{1,0:T(8,128)(2,1)} %feat_hbm.1, bf16[48,128,128]{2,1,0:T(8,128)(2,1)} %bitcast.2, bf16[1024,512]{1,0:T(8,128)(2,1)} %weight_hbm.1, f32[1,512]{1,0:T(1,128)} %bitcast.3), custom_call_target="tpu_custom_call" | custom-call | tf_op jit(solution)/shard_map/pallas_call | solution.py:395
  40.4 1.7 %copy.10 = bf16[256,512]{1,0:T(8,128)(2,1)} copy(bf16[256,512]{1,0:T(8,128)(2,1)} %shard_map.73) | data formatting | bytes 524288

commit v8 on v3

--- a/solution.py
+++ b/solution.py
@@ -9,7 +9,7 @@
 
 MESH = pl.DeviceIdType.MESH
 CHUNK = 128
-AHEAD = 2
+AHEAD = 3
 DENSE_LIMIT = 12 * 2**20
 
 
@@ -281,12 +281,12 @@
     send_rows(chunks)
 
     def stage(k, carry):
+        @pl.when(k + AHEAD < chunks)
+        def _():
+            send_own(k + AHEAD)
+
         for h in range(1, min(3, spots)):
             forward(k, h)
-
-        @pl.when(k + AHEAD < chunks)
-        def _():
-            send_own(k + AHEAD)
 
         for h in range(spots):
             if h > 2:

time: 38.8 us -> 40.2 us (1.036)
  Pallas kernels: 36.3 us -> 37.7 us
    pallas_call x1, Pallas kernels: 36.3 us -> 37.7 us  [per_device_fused(): pl.pallas_call(functools.partial(fused, rows_n, spots), out_shape=jax.Sha...]
where the time goes in v8:
time: 40.2 us; the launch traced here: 40.1 us
  Pallas kernels  37.7 us (94%)
  local copies, waits for them, and re-layouts  1.67 us (4%)
  between operations  0.66 us (2%)
    pallas_call x1, Pallas kernels, per_device_fused(): pl.pallas_call(functools.partial(fused, rows_n, spots), out_shape=jax.Sha...  37.7 us
    unnamed x1, local copies, waits for them, and re-layouts  1.67 us

profile of v8, /device:TPU:0, one launch (start us, length us, event | category | flops | bytes accessed | tf_op | source)
XLA Modules:
  0.0 40.1 jit_solution(14792818966825054995)
XLA Ops:
  0.7 37.7 %shard_map.73 = bf16[256,512]{1,0:T(8,128)(2,1)} custom-call(s32[1,1]{1,0:T(1,128)S(6)} %copy.9.live_hbm, s32[1,1,48]{2,1,0:T(1,128)} %src_hbm.1, s32[1,1,48]{2,1,0:T(1,128)} %dst_hbm.1, bf16[256,512]{1,0:T(8,128)(2,1)} %feat_hbm.1, bf16[48,128,128]{2,1,0:T(8,128)(2,1)} %bitcast.2, bf16[1024,512]{1,0:T(8,128)(2,1)} %weight_hbm.1, f32[1,512]{1,0:T(1,128)} %bitcast.3), custom_call_target="tpu_custom_call" | custom-call | tf_op jit(solution)/shard_map/pallas_call | solution.py:381
  38.4 1.7 %copy.10 = bf16[256,512]{1,0:T(8,128)(2,1)} copy(bf16[256,512]{1,0:T(8,128)(2,1)} %shard_map.73) | data formatting | bytes 524288

commit v9 on v4

--- a/solution.py
+++ b/solution.py
@@ -10,7 +10,7 @@
 MESH = pl.DeviceIdType.MESH
 CHUNK = 128
 AHEAD = 2
-FAR = 2
+FAR = 3
 DENSE_LIMIT = 12 * 2**20
 
 
@@ -281,35 +281,22 @@
         mixed[...] += jnp.dot(mean, part, preferred_element_type=jnp.float32)
 
     send_rows(chunks)
-    inner = (z > 0) & (z < spots - 1)
-
     def pass_on(k):
-        forward(k, 1)
+        for h in range(1, min(3, spots)):
+            forward(k, h)
 
         @pl.when(k + AHEAD < chunks)
         def _():
             send_own(k + AHEAD)
 
-        for h in range(2, min(3, spots)):
-            forward(k, h)
-
-    pass_on(0)
-
     def stage(k, carry):
-        @pl.when(inner & (k + 1 < chunks))
-        def _():
-            pass_on(k + 1)
-
+        pass_on(k)
         for h in range(spots):
             if h > 2:
                 forward(k, h)
             consume_at(k, h)
         send_buf[k] = acc[k].astype(jnp.bfloat16).reshape(rows_n, node_rows, CHUNK)
         send_rows(k)
-
-        @pl.when(jnp.logical_not(inner) & (k + 1 < chunks))
-        def _():
-            pass_on(k + 1)
 
         @pl.when(k == 0)
         def _():

time: 39.2 us -> 39.4 us (level)
  no operation moved by 1% of the time
where the time goes in v9:
time: 39.4 us; the launch traced here: 39.3 us
  Pallas kernels  37 us (94%)
  other arithmetic  1.67 us (4%)
  between operations  0.66 us (2%)
    pallas_call x1, Pallas kernels, per_device_fused(): pl.pallas_call(functools.partial(fused, rows_n, spots), out_shape=jax.Sha...  37 us
    max x1, other arithmetic, per_device_fused(): return jax.nn.relu(mixed)  1.67 us

profile of v9, /device:TPU:0, one launch (start us, length us, event | category | flops | bytes accessed | tf_op | source)
XLA Modules:
  0.0 39.3 jit_solution(15691011998315846593)
XLA Ops:
  0.7 37.0 %shard_map.73 = bf16[256,512]{1,0:T(8,128)(2,1)} custom-call(s32[1,1]{1,0:T(1,128)S(6)} %copy.8.live_hbm, s32[1,1,48]{2,1,0:T(1,128)} %src_hbm.1, s32[1,1,48]{2,1,0:T(1,128)} %dst_hbm.1, bf16[256,512]{1,0:T(8,128)(2,1)} %feat_hbm.1, bf16[48,128,128]{2,1,0:T(8,128)(2,1)} %bitcast.2, bf16[1024,512]{1,0:T(8,128)(2,1)} %weight_hbm.1, f32[1,512]{1,0:T(1,128)} %bitcast.3), custom_call_target="tpu_custom_call" | custom-call | tf_op jit(solution)/shard_map/pallas_call | solution.py:382
  37.6 1.7 %broadcast_maximum_fusion = bf16[256,512]{1,0:T(8,128)(2,1)} fusion(bf16[256,512]{1,0:T(8,128)(2,1)} %shard_map.73), kind=kLoop, calls=%fused_computation | loop fusion | flops 131072 | bytes 524288 | tf_op jit(solution)/shard_map/jit(relu)/max | solution.py:429
